TPU v7x, 128 devices: a whole 4x4x4 slice. The times are simulated.
128 devices in a mesh: expert: 32 (over z, x, core), fsdp: 4 (over y).
Axes of the slice: x: 4, y: 4, z: 4, core: 2. Of those that a mesh axis runs over, the one named last changes fastest.
Arguments:
- hidden: bfloat16 [24576, 1024], P(('expert', 'fsdp')), may hold values from -6 to 6
- segments: int32 [24576], P(('expert', 'fsdp')), may hold values from 0 to 2, as said below
- routes: int32 [24576, 8], P(('expert', 'fsdp')), may hold values from 0 to 31, all different within a row; in each aligned block of 192 rows (0 to 191, 192 to 383, ...) at most 72 rows name the same one
- attention_gain: bfloat16 [1024], P('fsdp'), may hold values from 0.25 to 1.75
- query_weight: bfloat16 [1024, 1024], P('fsdp'), may hold values from -0.1875 to 0.1875
- key_weight: bfloat16 [1024, 512], P('fsdp'), may hold values from -0.1875 to 0.1875
- value_weight: bfloat16 [1024, 512], P('fsdp'), may hold values from -0.1875 to 0.1875
- projection_weight: bfloat16 [1024, 1024], P('fsdp'), may hold values from -1 to 1
- mixture_gain: bfloat16 [1024], P('fsdp'), may hold values from 0.25 to 1.75
- router_weight: bfloat16 [1024, 32], P('fsdp'), may hold values from -0.09375 to 0.09375
- gate_weight: bfloat16 [32, 1024, 512], P('expert', 'fsdp'), may hold values from -0.1875 to 0.1875
- up_weight: bfloat16 [32, 1024, 512], P('expert', 'fsdp'), may hold values from -0.1875 to 0.1875
- down_weight: bfloat16 [32, 512, 1024], P('expert', 'fsdp'), may hold values from -1 to 1
- cotangent: bfloat16 [24576, 1024], P(('expert', 'fsdp')), may hold values from -6 to 6
Outputs:
- output: bfloat16 [24576, 1024], P(('expert', 'fsdp'))
- input_gradient: float32 [24576, 1024], P(('expert', 'fsdp'))
- attention_gain_gradient: float32 [1024], P('fsdp')
- query_gradient: float32 [1024, 1024], P('fsdp')
- key_gradient: float32 [1024, 512], P('fsdp')
- value_gradient: float32 [1024, 512], P('fsdp')
- projection_gradient: float32 [1024, 1024], P('fsdp')
- mixture_gain_gradient: float32 [1024], P('fsdp')
- router_gradient: float32 [1024, 32], P('fsdp')
- gate_gradient: float32 [32, 1024, 512], P('expert', 'fsdp')
- up_gradient: float32 [32, 1024, 512], P('expert', 'fsdp')
- down_gradient: float32 [32, 512, 1024], P('expert', 'fsdp')
Inputs may be any that keep to these rules, and one draw needn't show every extreme that they name: `segments`: within each sequence of 768 tokens the numbers never fall; number 1 begins within the sequence's first 192 tokens and number 2 within its last 192, so numbers 0 and 2 are never empty. `routes`: each row names 8 different experts; in the rows of one device (aligned blocks of 192 rows) no expert is named more than 72 times, a bound that some block reaches.
All inputs are finite; a program needn't handle non-finite values.
Results may differ from a plain program's by a relative error of at most 0.025.
Values may be sent and summed in bfloat16 or wider, within the bound.
No kernel may reach another device: no remote copies, remote signals or barrier semaphores. Data moves between devices by JAX's collectives and lax.ppermute only.
A program may use at most 192 MiB of HBM per device.

v0:
```python
import jax
import jax.numpy as jnp
from jax import lax
from jax.sharding import PartitionSpec as P

D = 1024
HEADS = 16
KV_HEADS = 8
HEAD = 64
FF = 512
TOP = 8


epsilon = 1e-06
base_theta = 10000.0


def rotary_tables(positions):
    halves = jnp.arange(HEAD // 2, dtype=jnp.int32).astype(jnp.float32)
    frequencies = base_theta ** (-2.0 * halves / HEAD)
    angles = positions.astype(jnp.float32)[:, None] * frequencies[None, :]
    angles = jnp.concatenate([angles, angles], axis=1)
    return (jnp.cos(angles)[:, None, :], jnp.sin(angles)[:, None, :])


def half_turn(values):
    first, second = jnp.split(values, 2, axis=-1)
    return jnp.concatenate([-second, first], axis=-1)


def rotate(values, cosines, sines):
    return values * cosines + half_turn(values) * sines


def rotate_back(deltas, cosines, sines):
    return deltas * cosines - half_turn(deltas * sines)


def normalize(values, gain):
    scaling = lax.rsqrt(jnp.mean(values * values, axis=-1, keepdims=True) + epsilon)
    return (values * scaling * gain, scaling)


def normalize_back(values, scaling, gain, deltas):
    inner = deltas * gain
    through = scaling * (
        inner - values * scaling * scaling * jnp.mean(inner * values, axis=-1, keepdims=True)
    )
    return (through, jnp.sum(deltas * values * scaling, axis=0))


def slot_tables(routes, expert_count, capacity):
    flat_routes = routes.reshape(-1)
    route_count = flat_routes.shape[0]
    onehot = (flat_routes[:, None] == jnp.arange(expert_count, dtype=jnp.int32)[None, :]).astype(
        jnp.int32
    )
    slot_rank = jnp.sum((jnp.cumsum(onehot, axis=0) - 1) * onehot, axis=1)
    target = flat_routes * capacity + slot_rank
    source = (
        jnp.full((expert_count * capacity,), route_count, jnp.int32)
        .at[target]
        .set(jnp.arange(route_count, dtype=jnp.int32))
    )
    return (source, target)


def contract_rows(left, right):
    return lax.dot_general(
        left, right, (((0,), (0,)), ((), ())), preferred_element_type=jnp.float32
    )


def contract_last(left, right):
    return lax.dot_general(
        left, right, (((1,), (1,)), ((), ())), preferred_element_type=jnp.float32
    )


def body(
    hidden,
    segments,
    routes,
    attention_gain,
    query_weight,
    key_weight,
    value_weight,
    projection_weight,
    mixture_gain,
    router_weight,
    gate_weight,
    up_weight,
    down_weight,
    cotangent,
):
    token_count = hidden.shape[0]
    fsdp_count = lax.axis_size("fsdp")
    sequence_size = token_count * fsdp_count
    expert_count = lax.axis_size("expert")
    capacity = min(token_count, 3 * token_count * TOP // (2 * expert_count))
    shared_width = KV_HEADS * HEAD
    head_share = HEADS // KV_HEADS
    scaling = HEAD ** (-0.5)
    gathered = (
        lax.all_gather(attention_gain, "fsdp", axis=0, tiled=True),
        lax.all_gather(query_weight, "fsdp", axis=0, tiled=True),
        lax.all_gather(key_weight, "fsdp", axis=0, tiled=True),
        lax.all_gather(value_weight, "fsdp", axis=0, tiled=True),
        lax.all_gather(projection_weight, "fsdp", axis=0, tiled=True),
        lax.all_gather(mixture_gain, "fsdp", axis=0, tiled=True),
        lax.all_gather(router_weight, "fsdp", axis=0, tiled=True),
        lax.all_gather(gate_weight, "fsdp", axis=1, tiled=True),
        lax.all_gather(up_weight, "fsdp", axis=1, tiled=True),
        lax.all_gather(down_weight, "fsdp", axis=1, tiled=True),
    )
    (
        gain_one,
        query_full,
        key_full,
        value_full,
        projection_full,
        gain_two,
        router_full,
        gate_full,
        up_full,
        down_full,
    ) = gathered
    gate_expert, up_expert, down_expert = (gate_full[0], up_full[0], down_full[0])
    positions = lax.axis_index("fsdp") * token_count + jnp.arange(token_count, dtype=jnp.int32)
    cosines, sines = rotary_tables(positions)
    residual = hidden.astype(jnp.float32)
    normed_one, scale_one = normalize(residual, gain_one.astype(jnp.float32))
    activations = normed_one.astype(jnp.bfloat16)
    query_linear = jnp.dot(activations, query_full, preferred_element_type=jnp.float32).reshape(
        token_count, HEADS, HEAD
    )
    key_linear = jnp.dot(activations, key_full, preferred_element_type=jnp.float32).reshape(
        token_count, KV_HEADS, HEAD
    )
    value_row_block = jnp.dot(activations, value_full, preferred_element_type=jnp.float32).astype(
        jnp.bfloat16
    )
    queries = rotate(query_linear, cosines, sines).astype(jnp.bfloat16)
    rotated_keys = (
        rotate(key_linear, cosines, sines).astype(jnp.bfloat16).reshape(token_count, shared_width)
    )
    marks = segments.astype(jnp.bfloat16)
    sequence_keys, sequence_values, sequence_marks = (
        lax.all_gather(rotated_keys, "fsdp", axis=0, tiled=True),
        lax.all_gather(value_row_block, "fsdp", axis=0, tiled=True),
        lax.all_gather(marks, "fsdp", axis=0, tiled=True),
    )
    visible = (jnp.arange(sequence_size, dtype=jnp.int32)[None, :] <= positions[:, None]) & (
        sequence_marks[None, :] == marks[:, None]
    )
    query_head_groups = queries.reshape(token_count, KV_HEADS, head_share, HEAD)
    key_head_tensor = sequence_keys.reshape(sequence_size, KV_HEADS, HEAD)
    value_head_tensor = sequence_values.reshape(sequence_size, KV_HEADS, HEAD)

    def score_rows():
        raw_scores = (
            jnp.einsum(
                "abyx,jbx->byaj",
                query_head_groups,
                key_head_tensor,
                preferred_element_type=jnp.float32,
            )
            * scaling
        )
        return jnp.where(visible[None, None], raw_scores, -1e30)

    scores = score_rows()
    row_max = jnp.max(scores, axis=-1, keepdims=True)
    weights = jnp.exp(scores - row_max)
    totals = jnp.sum(weights, axis=-1, keepdims=True)
    log_total = row_max + jnp.log(totals)
    attention_probabilities = (weights / totals).astype(jnp.bfloat16)
    mixed_rows = (
        jnp.einsum(
            "icav,vie->aice",
            attention_probabilities,
            value_head_tensor,
            preferred_element_type=jnp.float32,
        )
        .reshape(token_count, HEADS * HEAD)
        .astype(jnp.bfloat16)
    )
    residual_two = residual + jnp.dot(
        mixed_rows, projection_full, preferred_element_type=jnp.float32
    )
    normed_two, scale_two = normalize(residual_two, gain_two.astype(jnp.float32))
    expert_input = normed_two.astype(jnp.bfloat16)
    logits = jnp.dot(expert_input, router_full, preferred_element_type=jnp.float32)
    selectors = (
        routes[:, :, None] == jnp.arange(expert_count, dtype=jnp.int32)[None, None, :]
    ).astype(jnp.float32)
    chosen = jnp.sum(selectors * logits[:, None, :], axis=2)
    chosen_max = jnp.max(chosen, axis=1, keepdims=True)
    exponents = jnp.exp(chosen - chosen_max)
    gate_weights = exponents / jnp.sum(exponents, axis=1, keepdims=True)
    slot_source, slot_target = slot_tables(routes, expert_count, capacity)
    padded_input = jnp.concatenate([expert_input, jnp.zeros((1, D), jnp.bfloat16)], axis=0)
    outgoing = padded_input[slot_source // TOP].reshape(expert_count, capacity, D)
    arrived = lax.all_to_all(outgoing, "expert", split_axis=0, concat_axis=0, tiled=True)
    leading = arrived.shape[:2]
    flat_rows = arrived.reshape(-1, D)
    gate_values = jnp.dot(flat_rows, gate_expert, preferred_element_type=jnp.float32)
    up_values = jnp.dot(flat_rows, up_expert, preferred_element_type=jnp.float32)
    inner = (jax.nn.silu(gate_values) * up_values).astype(jnp.bfloat16)
    produced = jnp.dot(inner, down_expert, preferred_element_type=jnp.float32).astype(jnp.bfloat16)
    results = (
        produced.reshape(leading + (D,)),
        gate_values.reshape(leading + (FF,)),
        up_values.reshape(leading + (FF,)),
    )
    expert_results = results + (arrived,)
    returned = lax.all_to_all(expert_results[0], "expert", split_axis=0, concat_axis=0, tiled=True)
    route_outputs = (
        returned.reshape(expert_count * capacity, D)[slot_target]
        .reshape(token_count, TOP, D)
        .astype(jnp.float32)
    )
    output = (residual_two + jnp.sum(gate_weights[:, :, None] * route_outputs, axis=1)).astype(
        jnp.bfloat16
    )
    upstream = cotangent.astype(jnp.float32)
    gate_delta = jnp.sum(upstream[:, None, :] * route_outputs, axis=2)
    produced_delta = (
        (gate_weights[:, :, None] * upstream[:, None, :])
        .astype(jnp.bfloat16)
        .reshape(token_count * TOP, D)
    )
    padded_delta = jnp.concatenate([produced_delta, jnp.zeros((1, D), jnp.bfloat16)], axis=0)
    delta_outgoing = padded_delta[slot_source].reshape(expert_count, capacity, D)
    delta_arrived = lax.all_to_all(
        delta_outgoing, "expert", split_axis=0, concat_axis=0, tiled=True
    )
    arrived_rows = expert_results[3]
    flat_delta = delta_arrived.reshape(-1, D)
    flat_rows = arrived_rows.reshape(-1, D)
    gate_values = expert_results[1].reshape(-1, FF)
    up_values = expert_results[2].reshape(-1, FF)
    sigmoid_gate = jax.nn.sigmoid(gate_values)
    silu_gate = gate_values * sigmoid_gate
    inner = (silu_gate * up_values).astype(jnp.bfloat16)
    down_gradient = contract_rows(inner, flat_delta)
    inner_delta = contract_last(flat_delta, down_expert)
    gate_values_delta = (
        inner_delta * up_values * sigmoid_gate * (1.0 + gate_values * (1.0 - sigmoid_gate))
    ).astype(jnp.bfloat16)
    up_values_delta = (inner_delta * silu_gate).astype(jnp.bfloat16)
    gate_gradient = contract_rows(flat_rows, gate_values_delta)
    up_gradient = contract_rows(flat_rows, up_values_delta)
    rows_delta = (
        contract_last(gate_values_delta, gate_expert) + contract_last(up_values_delta, up_expert)
    ).astype(jnp.bfloat16)
    returned_delta = lax.all_to_all(
        rows_delta.reshape(expert_count, capacity, D),
        "expert",
        split_axis=0,
        concat_axis=0,
        tiled=True,
    )
    route_input_delta = (
        returned_delta.reshape(expert_count * capacity, D)[slot_target]
        .reshape(token_count, TOP, D)
        .astype(jnp.float32)
    )
    input_delta = jnp.sum(route_input_delta, axis=1)
    mean_delta = jnp.sum(gate_weights * gate_delta, axis=1, keepdims=True)
    chosen_delta = gate_weights * (gate_delta - mean_delta)
    logit_delta = jnp.sum(selectors * chosen_delta[:, :, None], axis=1).astype(jnp.bfloat16)
    router_gradient = contract_rows(expert_input, logit_delta)
    input_delta = input_delta + contract_last(logit_delta, router_full)
    residual_delta, mixture_gradient = normalize_back(
        residual_two, scale_two, gain_two.astype(jnp.float32), input_delta
    )
    residual_delta = residual_delta + upstream
    attention_delta = residual_delta.astype(jnp.bfloat16)
    projection_gradient = contract_rows(mixed_rows, attention_delta)
    mixed_output_delta = (
        contract_last(attention_delta, projection_full)
        .astype(jnp.bfloat16)
        .reshape(token_count, KV_HEADS, head_share, HEAD)
    )
    unrounded = jnp.exp(score_rows() - log_total)
    probability_delta = jnp.einsum(
        "abyx,jbx->byaj", mixed_output_delta, value_head_tensor, preferred_element_type=jnp.float32
    )
    row_delta = jnp.sum(probability_delta * unrounded, axis=-1, keepdims=True)
    attention_score_delta = (unrounded * (probability_delta - row_delta)).astype(jnp.bfloat16)
    query_delta = (
        jnp.einsum(
            "icav,vie->aice",
            attention_score_delta,
            key_head_tensor,
            preferred_element_type=jnp.float32,
        ).reshape(token_count, HEADS, HEAD)
        * scaling
    )
    key_partial = (
        jnp.einsum(
            "lapf,play->fly",
            attention_score_delta,
            query_head_groups,
            preferred_element_type=jnp.float32,
        )
        * scaling
    )
    value_partial = jnp.einsum(
        "lapf,play->fly",
        attention_probabilities,
        mixed_output_delta,
        preferred_element_type=jnp.float32,
    )
    key_own, value_own = (
        lax.psum_scatter(
            key_partial.reshape(sequence_size, shared_width).astype(jnp.bfloat16),
            "fsdp",
            scatter_dimension=0,
            tiled=True,
        ).astype(jnp.float32),
        lax.psum_scatter(
            value_partial.reshape(sequence_size, shared_width).astype(jnp.bfloat16),
            "fsdp",
            scatter_dimension=0,
            tiled=True,
        ).astype(jnp.float32),
    )
    query_linear_delta = (
        rotate_back(query_delta, cosines, sines)
        .reshape(token_count, HEADS * HEAD)
        .astype(jnp.bfloat16)
    )
    key_linear_delta = (
        rotate_back(key_own.reshape(token_count, KV_HEADS, HEAD), cosines, sines)
        .reshape(token_count, shared_width)
        .astype(jnp.bfloat16)
    )
    values_delta = value_own.astype(jnp.bfloat16)
    query_gradient = contract_rows(activations, query_linear_delta)
    key_gradient = contract_rows(activations, key_linear_delta)
    value_gradient = contract_rows(activations, values_delta)
    activation_delta = (
        contract_last(query_linear_delta, query_full)
        + contract_last(key_linear_delta, key_full)
        + contract_last(values_delta, value_full)
    )
    first_delta, attention_gradient = normalize_back(
        residual, scale_one, gain_one.astype(jnp.float32), activation_delta
    )
    input_gradient = residual_delta + first_delta
    summed = (
        lax.psum_scatter(
            attention_gradient.astype(jnp.bfloat16), "fsdp", scatter_dimension=0, tiled=True
        ).astype(jnp.float32),
        lax.psum_scatter(
            query_gradient.astype(jnp.bfloat16), "fsdp", scatter_dimension=0, tiled=True
        ).astype(jnp.float32),
        lax.psum_scatter(
            key_gradient.astype(jnp.bfloat16), "fsdp", scatter_dimension=0, tiled=True
        ).astype(jnp.float32),
        lax.psum_scatter(
            value_gradient.astype(jnp.bfloat16), "fsdp", scatter_dimension=0, tiled=True
        ).astype(jnp.float32),
        lax.psum_scatter(
            projection_gradient.astype(jnp.bfloat16), "fsdp", scatter_dimension=0, tiled=True
        ).astype(jnp.float32),
        lax.psum_scatter(
            mixture_gradient.astype(jnp.bfloat16), "fsdp", scatter_dimension=0, tiled=True
        ).astype(jnp.float32),
        lax.psum_scatter(
            router_gradient.astype(jnp.bfloat16), "fsdp", scatter_dimension=0, tiled=True
        ).astype(jnp.float32),
        lax.psum_scatter(
            gate_gradient[None].astype(jnp.bfloat16), "fsdp", scatter_dimension=1, tiled=True
        ).astype(jnp.float32),
        lax.psum_scatter(
            up_gradient[None].astype(jnp.bfloat16), "fsdp", scatter_dimension=1, tiled=True
        ).astype(jnp.float32),
        lax.psum_scatter(
            down_gradient[None].astype(jnp.bfloat16), "fsdp", scatter_dimension=1, tiled=True
        ).astype(jnp.float32),
    )
    replicated = (
        lax.psum(summed[0].astype(jnp.bfloat16), "expert").astype(jnp.float32),
        lax.psum(summed[1].astype(jnp.bfloat16), "expert").astype(jnp.float32),
        lax.psum(summed[2].astype(jnp.bfloat16), "expert").astype(jnp.float32),
        lax.psum(summed[3].astype(jnp.bfloat16), "expert").astype(jnp.float32),
        lax.psum(summed[4].astype(jnp.bfloat16), "expert").astype(jnp.float32),
        lax.psum(summed[5].astype(jnp.bfloat16), "expert").astype(jnp.float32),
        lax.psum(summed[6].astype(jnp.bfloat16), "expert").astype(jnp.float32),
    )
    expert_summed = (summed[7], summed[8], summed[9])
    return (
        output,
        input_gradient,
        replicated[0],
        replicated[1],
        replicated[2],
        replicated[3],
        replicated[4],
        replicated[5],
        replicated[6],
        expert_summed[0],
        expert_summed[1],
        expert_summed[2],
    )


def solution(mesh):
    placed = (
        P(("expert", "fsdp"), None),
        P(("expert", "fsdp")),
        P(("expert", "fsdp"), None),
        P("fsdp"),
        P("fsdp", None),
        P("fsdp", None),
        P("fsdp", None),
        P("fsdp", None),
        P("fsdp"),
        P("fsdp", None),
        P("expert", "fsdp", None),
        P("expert", "fsdp", None),
        P("expert", "fsdp", None),
        P(("expert", "fsdp"), None),
    )
    return jax.shard_map(
        body,
        mesh=mesh,
        in_specs=placed,
        out_specs=(
            P(("expert", "fsdp"), None),
            P(("expert", "fsdp"), None),
            P("fsdp"),
            P("fsdp", None),
            P("fsdp", None),
            P("fsdp", None),
            P("fsdp", None),
            P("fsdp"),
            P("fsdp", None),
            P("expert", "fsdp", None),
            P("expert", "fsdp", None),
            P("expert", "fsdp", None),
        ),
        check_vma=False,
    )
```

profile of v0, /device:TPU:0, one launch (start us, length us, event | category | flops | bytes accessed | tf_op | source)
XLA Modules:
  0.0 850.4 jit_solution(15146132034905622751)
XLA Ops:
  17.2 10.9 %all-reduce.2 = bf16[768]{0:T(1024)(128)(2,1)S(1)} all-reduce(bf16[768]{0:T(1024)(128)(2,1)S(1)} %dynamic-update-slice), channel_id=1, replica_groups=mesh['expert'=32,'fsdp'=4] {'fsdp'}, use_global_device_ids=true, to_apply=%add.2 | all-reduce | flops 768 | bytes 3072
  35.1 9.0 %all-gather = bf16[4,1,256]{2,1,0:T(2,128)(2,1)S(1)} all-gather(bf16[1,1,256]{2,1,0:T(2,128)(2,1)S(1)} %reshape.474), channel_id=1, replica_groups=mesh['expert'=32,'fsdp'=4] {'fsdp'}, dimensions={0}, use_global_device_ids=true | all-gather | bytes 2560 | tf_op jit(solution)/shard_map/all_gather | solution.py:105
  45.2 9.1 %reduce-window.6 = s32[32,12,128]{2,1,0:T(8,128)S(1)} reduce-window(s32[32,12,128]{2,1,0:T(8,128)S(1)} %fusion.40, s32[]{:T(128)} %constant.65.clone.1), window={size=1x1x128 pad=0_0x0_0x127_0}, to_apply=%region_7.8 | reduce-window | flops 6242304 | bytes 393220 | tf_op jit(solution)/shard_map/reduce-window
  64.6 14.2 %all_gather.44 = bf16[768,512]{1,0:T(8,128)(2,1)S(1)} all-gather(bf16[192,512]{1,0:T(8,128)(2,1)S(1)} %add_convert_fusion.2), channel_id=1, replica_groups=mesh['expert'=32,'fsdp'=4] {'fsdp'}, dimensions={0}, use_global_device_ids=true | all-gather | bytes 983040 | tf_op jit(solution)/shard_map/all_gather | solution.py:149
  81.0 16.6 %all_gather.41 = bf16[768,512]{1,0:T(8,128)(2,1)S(1)} all-gather(bf16[192,512]{1,0:T(8,128)(2,1)S(1)} %convolution_convert_fusion.10), channel_id=1, replica_groups=mesh['expert'=32,'fsdp'=4] {'fsdp'}, dimensions={0}, use_global_device_ids=true | all-gather | bytes 983040 | tf_op jit(solution)/shard_map/all_gather | solution.py:150
  115.7 18.9 %all-gather.16.cloned.1.call-done = bf16[1024,1024]{1,0:T(8,128)(2,1)} async-done(((bf16[256,1024]{1,0:T(8,128)(2,1)}), bf16[1024,1024]{1,0:T(8,128)(2,1)}) %all-gather.16.cloned.1.call-update) | async-done | bytes 2097168 | tf_op jit(solution)/shard_map/all_gather | solution.py:109
  154.3 11.9 %all_gather.48 = bf16[1024,32]{0,1:T(8,128)(2,1)S(1)} all-gather(bf16[256,32]{0,1:T(8,128)(2,1)S(1)} %copy-done.57), channel_id=1, replica_groups=mesh['expert'=32,'fsdp'=4] {'fsdp'}, dimensions={0}, use_global_device_ids=true | all-gather | bytes 81920 | tf_op jit(solution)/shard_map/all_gather | solution.py:111
  177.8 35.6 %all-to-all-done = bf16[32,72,1024]{2,1,0:T(8,128)(2,1)} async-done(((bf16[32,72,1024]{2,1,0:T(8,128)(2,1)}), bf16[32,72,1024]{2,1,0:T(8,128)(2,1)}, u32[]{:S(2)}, u32[]{:S(2)}) %all-to-all-start) | async-done | bytes 4718624 | tf_op jit(solution)/shard_map/all_to_all | solution.py:204
  227.0 17.5 %all-gather.18.cloned.1.call-done = bf16[1,1024,512]{2,1,0:T(8,128)(2,1)} async-done(((bf16[1,256,512]{2,1,0:T(8,128)(2,1)}), bf16[1,1024,512]{2,1,0:T(8,128)(2,1)}) %all-gather.18.cloned.1.call-update) | async-done | bytes 1048592 | tf_op jit(solution)/shard_map/all_gather | solution.py:112
  251.9 18.6 %all-gather.22.cloned.1.call-done = bf16[1,512,1024]{2,1,0:T(8,128)(2,1)} async-done(((bf16[1,128,1024]{2,1,0:T(8,128)(2,1)}), bf16[1,512,1024]{2,1,0:T(8,128)(2,1)}) %all-gather.22.cloned.1.call-update) | async-done | bytes 1048592 | tf_op jit(solution)/shard_map/all_gather | solution.py:114
  278.0 12.4 %multiply_convert_fusion = (bf16[2304,512]{1,0:T(8,128)(2,1)}, bf16[2304,512]{1,0:T(8,128)(2,1)}, bf16[2304,512]{1,0:T(8,128)(2,1)S(1)}) fusion(f32[2304,512]{1,0:T(8,128)} %fusion.25, f32[2304,512]{1,0:T(8,128)} %fusion.21, bf16[2304,1024]{1,0:T(8,128)(2,1)} %bitcast.31, bf16[1,512,1024]{2,1,0:T(8,128)(2,1)} %all-gather.22.cloned.1.call-done), kind=kOutput, calls=%fused_computation.25 | convolution fusion | flops 2433613824 | bytes 22282240 | tf_op jit(solution)/shard_map/dot_general | solution.py:75
  308.6 50.8 %all-to-all-done.1 = bf16[32,72,1024]{2,1,0:T(8,128)(2,1)} async-done(((bf16[32,72,1024]{2,1,0:T(8,128)(2,1)}), bf16[32,72,1024]{2,1,0:T(8,128)(2,1)}, u32[]{:S(2)}, u32[]{:S(2)}) %all-to-all-start.1) | async-done | bytes 4718624 | tf_op jit(solution)/shard_map/all_to_all | solution.py:217
  365.2 10.0 %gather_fusion.1 = bf16[1536,1024]{1,0:T(8,128)(2,1)S(1)} fusion(bf16[2304,1024]{1,0:T(8,128)(2,1)} %bitcast.27, s32[2048]{0:T(1024)S(1)} %pad_clamp_fusion.2), kind=kCustom, calls=%fused_computation.1 | custom fusion | bytes 6297600 | tf_op jit(solution)/shard_map/gather | solution.py:219
  382.6 41.6 %all-to-all-done.3 = bf16[32,72,1024]{2,1,0:T(8,128)(2,1)} async-done(((bf16[32,72,1024]{2,1,0:T(8,128)(2,1)}), bf16[32,72,1024]{2,1,0:T(8,128)(2,1)}, u32[]{:S(2)}, u32[]{:S(2)}) %all-to-all-start.3) | async-done | bytes 4718624 | tf_op jit(solution)/shard_map/all_to_all | solution.py:257
  424.2 10.9 %gather_fusion.3 = bf16[1536,1024]{1,0:T(8,128)(2,1)} fusion(bf16[2304,1024]{1,0:T(8,128)(2,1)} %bitcast.33, s32[2048]{0:T(1024)} %copy-done.48), kind=kCustom, calls=%fused_computation.3 | custom fusion | bytes 6297600 | tf_op jit(solution)/shard_map/gather | solution.py:265
  504.1 11.6 %reduce-scatter.29.cloned.1.call-done = bf16[1,128,1024]{2,1,0:T(8,128)(2,1)} async-done(((bf16[1,512,1024]{2,1,0:T(8,128)(2,1)}), bf16[1,128,1024]{2,1,0:T(8,128)(2,1)}) %reduce-scatter.29.cloned.1.call-update) | async-done | bytes 262160 | tf_op jit(solution)/shard_map/reduce_scatter | solution.py:381
  517.5 23.9 %reduce-scatter.27.cloned.1.call-done = bf16[1,256,512]{2,1,0:T(8,128)(2,1)} async-done(((bf16[1,1024,512]{2,1,0:T(8,128)(2,1)}), bf16[1,256,512]{2,1,0:T(8,128)(2,1)}) %reduce-scatter.27.cloned.1.call-update) | async-done | bytes 262160 | tf_op jit(solution)/shard_map/reduce_scatter | solution.py:378
  543.2 23.8 %reduce-scatter.25.cloned.1.call-done = bf16[1,256,512]{2,1,0:T(8,128)(2,1)} async-done(((bf16[1,1024,512]{2,1,0:T(8,128)(2,1)}), bf16[1,256,512]{2,1,0:T(8,128)(2,1)}) %reduce-scatter.25.cloned.1.call-update) | async-done | bytes 262160 | tf_op jit(solution)/shard_map/reduce_scatter | solution.py:375
  573.6 19.8 %reduce-scatter.19.cloned.1.call-done = bf16[256,512]{1,0:T(8,128)(2,1)} async-done(((bf16[1024,512]{1,0:T(8,128)(2,1)}), bf16[256,512]{1,0:T(8,128)(2,1)}) %reduce-scatter.19.cloned.1.call-update) | async-done | bytes 262160 | tf_op jit(solution)/shard_map/reduce_scatter | solution.py:363
  593.4 26.2 %reduce-scatter.17.cloned.1.call-done = bf16[256,512]{1,0:T(8,128)(2,1)} async-done(((bf16[1024,512]{1,0:T(8,128)(2,1)}), bf16[256,512]{1,0:T(8,128)(2,1)}) %reduce-scatter.17.cloned.1.call-update) | async-done | bytes 262160 | tf_op jit(solution)/shard_map/reduce_scatter | solution.py:360
  619.6 31.8 %reduce-scatter.21.cloned.1.call-done = bf16[256,1024]{1,0:T(8,128)(2,1)} async-done(((bf16[1024,1024]{1,0:T(8,128)(2,1)}), bf16[256,1024]{1,0:T(8,128)(2,1)}) %reduce-scatter.21.cloned.1.call-update) | async-done | bytes 524304 | tf_op jit(solution)/shard_map/reduce_scatter | solution.py:366
  651.4 31.7 %reduce-scatter.15.cloned.1.call-done = bf16[256,1024]{1,0:T(8,128)(2,1)} async-done(((bf16[1024,1024]{1,0:T(8,128)(2,1)}), bf16[256,1024]{1,0:T(8,128)(2,1)}) %reduce-scatter.15.cloned.1.call-update) | async-done | bytes 524304 | tf_op jit(solution)/shard_map/reduce_scatter | solution.py:357
  694.0 12.0 %reduce-scatter.23.cloned.1.call-done = bf16[256,32]{0,1:T(8,128)(2,1)} async-done(((bf16[1024,32]{0,1:T(8,128)(2,1)}), bf16[256,32]{0,1:T(8,128)(2,1)}) %reduce-scatter.23.cloned.1.call-update) | async-done | bytes 16400 | tf_op jit(solution)/shard_map/reduce_scatter | solution.py:372
  706.1 126.3 %all-reduce.5 = (bf16[256]{0:T(256)(128)(2,1)S(1)}, bf16[256]{0:T(256)(128)(2,1)S(1)}, bf16[256,32]{0,1:T(8,128)(2,1)S(1)}) all-reduce(bf16[256]{0:T(256)(128)(2,1)S(1)} %dynamic-slice.2, bf16[256]{0:T(256)(128)(2,1)S(1)} %dynamic-slice.4, ...), channel_id=1, replica_groups=mesh['expert'=32,'fsdp'=4] {'expert'}, use_global_device_ids=true, to_apply=%region_23.24 | all-reduce | flops 8704 | bytes 34816 | tf_op jit(solution)/shard_map/psum | solution.py:386
  (314 shorter events, 237.9 us)
Async XLA Ops:
  7.2 55.1 %all-gather.12.cloned.1.call-start = ((), (), s32[]{:S(2)}) async-start(), calls=%async_computation.15 | async-start | bytes 1310720 | tf_op jit(solution)/shard_map/all_gather | solution.py:107
  7.9 71.2 %all-gather.10.cloned.1.call-start = ((), (), s32[]{:S(2)}) async-start(), calls=%async_computation.14 | async-start | bytes 1310720 | tf_op jit(solution)/shard_map/all_gather | solution.py:108
  8.7 92.4 %all-gather.14.cloned.1.call-start = ((), (), s32[]{:S(2)}) async-start(), calls=%async_computation.16 | async-start | bytes 2621440 | tf_op jit(solution)/shard_map/all_gather | solution.py:106
  9.4 125.2 %all-gather.16.cloned.1.call-start = ((), (), s32[]{:S(2)}) async-start(), calls=%async_computation.17 | async-start | bytes 2621440 | tf_op jit(solution)/shard_map/all_gather | solution.py:109
  14.9 86.2 %copy-start.51 = (f32[192]{0:T(256)}, f32[192]{0:T(256)S(1)}, u32[]{:S(2)}) copy-start(f32[192]{0:T(256)S(1)} %add_rsqrt_fusion.1) | copy-start | bytes 2308
  35.1 101.9 %copy-start.49 = (f32[4,1,256]{2,1,0:T(1,128)}, f32[4,1,256]{2,1,0:T(1,128)S(1)}, u32[]{:S(2)}) copy-start(f32[4,1,256]{2,1,0:T(1,128)S(1)} %convert_element_type.296) | copy-start | bytes 12292
  146.1 67.2 %all-to-all-start = ((bf16[32,72,1024]{2,1,0:T(8,128)(2,1)}), bf16[32,72,1024]{2,1,0:T(8,128)(2,1)}, u32[]{:S(2)}, u32[]{:S(2)}) async-start(bf16[32,72,1024]{2,1,0:T(8,128)(2,1)} %bitcast.194), calls=%async_computation | async-start | bytes 9437184 | tf_op jit(solution)/shard_map/all_to_all | solution.py:204
  153.6 66.0 %all-gather.20.cloned.1.call-start = ((), (), s32[]{:S(2)}) async-start(), calls=%async_computation.19 | async-start | bytes 1310720 | tf_op jit(solution)/shard_map/all_gather | solution.py:113
  213.3 64.6 %all-to-all-start.2 = ((bf16[32,72,1024]{2,1,0:T(8,128)(2,1)}), bf16[32,72,1024]{2,1,0:T(8,128)(2,1)}, u32[]{:S(2)}, u32[]{:S(2)}) async-start(bf16[32,72,1024]{2,1,0:T(8,128)(2,1)} %bitcast.193), calls=%async_computation.2 | async-start | bytes 9437184 | tf_op jit(solution)/shard_map/all_to_all | solution.py:235
  218.2 26.3 %all-gather.18.cloned.1.call-start = ((), (), s32[]{:S(2)}) async-start(), calls=%async_computation.18 | async-start | bytes 1310720 | tf_op jit(solution)/shard_map/all_gather | solution.py:112
  218.8 51.7 %all-gather.22.cloned.1.call-start = ((), (), s32[]{:S(2)}) async-start(), calls=%async_computation.20 | async-start | bytes 1310720 | tf_op jit(solution)/shard_map/all_gather | solution.py:114
  294.6 64.9 %all-to-all-start.1 = ((bf16[32,72,1024]{2,1,0:T(8,128)(2,1)}), bf16[32,72,1024]{2,1,0:T(8,128)(2,1)}, u32[]{:S(2)}, u32[]{:S(2)}) async-start(bf16[32,72,1024]{2,1,0:T(8,128)(2,1)} %bitcast.206), calls=%async_computation.1 | async-start | bytes 9437184 | tf_op jit(solution)/shard_map/all_to_all | solution.py:217
  359.5 64.7 %all-to-all-start.3 = ((bf16[32,72,1024]{2,1,0:T(8,128)(2,1)}), bf16[32,72,1024]{2,1,0:T(8,128)(2,1)}, u32[]{:S(2)}, u32[]{:S(2)}) async-start(bf16[32,72,1024]{2,1,0:T(8,128)(2,1)} %bitcast.205), calls=%async_computation.3 | async-start | bytes 9437184 | tf_op jit(solution)/shard_map/all_to_all | solution.py:257
  364.5 117.8 %reduce-scatter.33.cloned.1.call-start = ((), (), s32[]{:S(2)}) async-start(), calls=%async_computation.30 | async-start | bytes 983040
  447.0 43.1 %reduce-scatter.31.cloned.1.call-start = ((), (), s32[]{:S(2)}) async-start(), calls=%async_computation.29 | async-start | bytes 983040
  461.7 54.1 %reduce-scatter.29.cloned.1.call-start = ((), (), s32[]{:S(2)}) async-start(), calls=%async_computation.28 | async-start | bytes 1310720 | tf_op jit(solution)/shard_map/reduce_scatter | solution.py:381
  468.4 73.0 %reduce-scatter.27.cloned.1.call-start = ((), (), s32[]{:S(2)}) async-start(), calls=%async_computation.27 | async-start | bytes 1310720 | tf_op jit(solution)/shard_map/reduce_scatter | solution.py:378
  475.2 91.8 %reduce-scatter.25.cloned.1.call-start = ((), (), s32[]{:S(2)}) async-start(), calls=%async_computation.26 | async-start | bytes 1310720 | tf_op jit(solution)/shard_map/reduce_scatter | solution.py:375
  482.2 111.2 %reduce-scatter.19.cloned.1.call-start = ((), (), s32[]{:S(2)}) async-start(), calls=%async_computation.23 | async-start | bytes 1310720 | tf_op jit(solution)/shard_map/reduce_scatter | solution.py:363
  484.8 134.8 %reduce-scatter.17.cloned.1.call-start = ((), (), s32[]{:S(2)}) async-start(), calls=%async_computation.22 | async-start | bytes 1310720 | tf_op jit(solution)/shard_map/reduce_scatter | solution.py:360
  493.7 157.8 %reduce-scatter.21.cloned.1.call-start = ((), (), s32[]{:S(2)}) async-start(), calls=%async_computation.24 | async-start | bytes 2621440 | tf_op jit(solution)/shard_map/reduce_scatter | solution.py:366
  495.8 187.3 %reduce-scatter.15.cloned.1.call-start = ((), (), s32[]{:S(2)}) async-start(), calls=%async_computation.21 | async-start | bytes 2621440 | tf_op jit(solution)/shard_map/reduce_scatter | solution.py:357
  503.3 202.8 %reduce-scatter.23.cloned.1.call-start = ((), (), s32[]{:S(2)}) async-start(), calls=%async_computation.25 | async-start | bytes 81920 | tf_op jit(solution)/shard_map/reduce_scatter | solution.py:372
  569.7 265.6 %all-reduce.10.cloned.1.call-start = ((), (), s32[]{:S(2)}) async-start(), calls=%async_computation.31 | async-start | bytes 3145728 | tf_op jit(solution)/shard_map/psum | solution.py:387
  (66 other events, 1022.4 us)
Sparse Core Ops, SparseCore 0:
  9.7 26.4 all-gather.11
  37.9 24.5 all-gather.9
  64.1 36.9 all-gather.13
  102.6 31.9 all-gather.15
  155.8 24.0 all-gather.19
  220.4 24.0 all-gather.17
  246.2 24.2 all-gather.21
  447.1 17.6 reduce-scatter.32
  467.8 22.2 reduce-scatter.30
  492.3 23.3 reduce-scatter.28
  518.2 23.1 reduce-scatter.26
  543.7 23.2 reduce-scatter.24
  570.1 23.2 reduce-scatter.18
  596.2 23.3 reduce-scatter.16
  622.0 29.4 reduce-scatter.20
  653.7 29.3 reduce-scatter.14
  686.0 20.0 reduce-scatter.22
  709.6 106.4 all-reduce.9
where the time goes:
time: 856 us; the launch traced here: 850 us
  waiting for transfers between devices  384 us (45%)
  blocking collectives  204 us (24%)
  matrix products  105 us (12%)
  local copies, waits for them, and re-layouts  64.3 us (8%)
  other arithmetic  51.7 us (6%)
  starting transfers between devices  24.2 us (3%)
  between operations  17.3 us (2%)
    psum x1, blocking collectives, body(): lax.psum(summed[0].astype(jnp.bfloat16), 'expert').astype(jnp.float32)  126 us
    all_to_all x1, waiting for transfers between devices, body(): lax.all_to_all(expert_results[0], 'expert', split_axis=0, concat_axis=0,...  50.8 us
    all_to_all x1, waiting for transfers between devices, body(): lax.all_to_all(rows_delta.reshape(expert_count, capacity, D), 'expert', s...  41.6 us
    all_to_all x1, waiting for transfers between devices, body(): lax.all_to_all(outgoing, 'expert', split_axis=0, concat_axis=0, tiled=True)  35.6 us
    reduce_scatter x1, waiting for transfers between devices, body(): lax.psum_scatter(projection_gradient.astype(jnp.bfloat16), 'fsdp', scatte...  31.8 us
    reduce_scatter x1, waiting for transfers between devices, body(): lax.psum_scatter(query_gradient.astype(jnp.bfloat16), 'fsdp', scatter_dim...  31.7 us
    dot_general x8, matrix products, contract_rows(): lax.dot_general(left, right, (((0,), (0,)), ((), ())), preferred_element_...  29.4 us
    dot_general x8, matrix products, contract_last(): lax.dot_general(left, right, (((1,), (1,)), ((), ())), preferred_element_...  28.6 us
  transfers between devices with their start and end apart: 22, of which 17 were waited for; matrix products, arithmetic and copies ran while one was open for 18% of the time, Pallas kernels for 0%

commit v1 on v0

v1 whole, which is shorter than its diff:
```python
import jax
import jax.numpy as jnp
from jax import lax
from jax.experimental import pallas as pl
from jax.experimental.pallas import tpu as pltpu
from jax.sharding import PartitionSpec as P

D = 1024
HEADS = 16
KV_HEADS = 8
HEAD = 64
FF = 512
TOP = 8
EXPERTS = 32
TOK = 192
CAP = 72
RING = 4

epsilon = 1e-06
base_theta = 10000.0
bf16 = jnp.bfloat16
f32 = jnp.float32


def place(z, x, core):
    return (z * RING + x) * 2 + core


def plane_perm(line, shift):
    pairs = []
    for z in range(RING):
        for x in range(RING):
            for core in range(2):
                if (core == 0) == (line == 0):
                    to = place(z, (x + shift) % RING, core)
                else:
                    to = place((z + shift) % RING, x, core)
                pairs.append((place(z, x, core), to))
    return pairs


def send_plane(value, line, shift):
    return lax.ppermute(value, "expert", plane_perm(line, shift % RING))


def send_core(value):
    return lax.ppermute(value, "expert", [(i, i ^ 1) for i in range(EXPERTS)])


def send_y(value, shift):
    return lax.ppermute(value, "fsdp", [(i, (i + shift) % RING) for i in range(RING)])


def dot(left, right):
    return jnp.dot(left, right, preferred_element_type=f32)


def contract_rows(left, right):
    return lax.dot_general(left, right, (((0,), (0,)), ((), ())), preferred_element_type=f32)


def contract_last(left, right):
    return lax.dot_general(left, right, (((1,), (1,)), ((), ())), preferred_element_type=f32)


def half_turn(values):
    first, second = jnp.split(values, 2, axis=-1)
    return jnp.concatenate([-second, first], axis=-1)


def rotate(values, cosines, sines):
    return values * cosines + half_turn(values) * sines


def rotate_back(deltas, cosines, sines):
    return deltas * cosines - half_turn(deltas * sines)


def scale_of(values):
    return lax.rsqrt(jnp.mean(values * values, axis=-1, keepdims=True) + epsilon)


def pick(blocks, index):
    return lax.dynamic_index_in_dim(blocks, index, 0, keepdims=False)


def in_order(received, position):
    own, one, two, three = received
    line = jnp.stack([three, two, one, own, three, two, one])
    return lax.dynamic_slice_in_dim(line, (3 - position) % RING, RING, 0)


def expert_kernel(groups, *refs):
    count = len(groups)
    x_refs, c_refs = refs[:count], refs[count : 2 * count]
    (slot_lane, slot_col, gate_lane, gate_w, up_w, down_w) = refs[2 * count : 2 * count + 6]
    outs = refs[2 * count + 6 :]
    delta_refs = outs[:count]
    gd_ref, xs_ref, cs_ref, inner_ref, dg_ref, du_ref = outs[count:]
    sources = [(g, k) for g in range(count) for k in range(groups[g])]
    rows = 2 * CAP
    slot_at = lax.broadcasted_iota(jnp.int32, (rows, TOK), 0)
    lane_at = lax.broadcasted_iota(jnp.int32, (TOK, rows), 1)
    picks, x_parts, c_parts, weights = [], [], [], []
    for s, (g, k) in enumerate(sources):
        first, second = slot_lane[s, 0:1, :], slot_lane[s, 1:2, :] + CAP
        upper = slot_at < CAP
        chosen_f = (slot_at == jnp.where(upper, first, second)).astype(f32)
        weight = jnp.where(upper, gate_lane[s, 0:1, :], gate_lane[s, 1:2, :])
        weights.append(jnp.sum(chosen_f * weight, axis=1, keepdims=True))
        picks.append(chosen_f)
        chosen_b = chosen_f.astype(bf16)
        x_parts.append(dot(chosen_b, x_refs[g][k * TOK : (k + 1) * TOK, :]))
        c_parts.append(dot(chosen_b, c_refs[g][k * TOK : (k + 1) * TOK, :]))
    back = []
    for e in range(2):
        span = slice(e * CAP, (e + 1) * CAP)
        xs = jnp.concatenate([part[span] for part in x_parts], axis=0).astype(bf16)
        cs = jnp.concatenate([part[span] for part in c_parts], axis=0).astype(bf16)
        weight = jnp.concatenate([part[span] for part in weights], axis=0)
        xs_ref[e] = xs
        cs_ref[e] = cs
        gate_values = dot(xs, gate_w[e])
        up_values = dot(xs, up_w[e])
        inner_delta = contract_last(cs, down_w[e])
        sigmoid = jax.nn.sigmoid(gate_values)
        silu = gate_values * sigmoid
        inner = silu * up_values
        gate_delta = jnp.sum(inner * inner_delta, axis=1, keepdims=True)
        inner_ref[e] = (inner * weight).astype(bf16)
        inner_delta = inner_delta * weight
        dg = (inner_delta * up_values * sigmoid * (1.0 + gate_values * (1.0 - sigmoid))).astype(bf16)
        du = (inner_delta * silu).astype(bf16)
        dg_ref[e] = dg
        du_ref[e] = du
        back.append(contract_last(dg, gate_w[e]) + contract_last(du, up_w[e]))
        for s in range(len(sources)):
            own = picks[s][span] * gate_delta[s * CAP : (s + 1) * CAP]
            gd_ref[s, e : e + 1, :] = jnp.sum(own, axis=0, keepdims=True)
    for s, (g, k) in enumerate(sources):
        first, second = slot_col[s, :, 0:1], slot_col[s, :, 1:2] + CAP
        scatter = (lane_at == jnp.where(lane_at < CAP, first, second)).astype(f32).astype(bf16)
        span = slice(s * CAP, (s + 1) * CAP)
        part = jnp.concatenate([back[0][span], back[1][span]], axis=0).astype(bf16)
        delta_refs[g][k * TOK : (k + 1) * TOK, :] = dot(scatter, part).astype(bf16)


def expert_call(xs, cs, slot_lane, slot_col, gate_lane, gate_w, up_w, down_w):
    groups = tuple(x.shape[0] // TOK for x in xs)
    sources = sum(groups)
    slots = sources * CAP
    shapes = [jax.ShapeDtypeStruct(x.shape, bf16) for x in xs]
    shapes += [
        jax.ShapeDtypeStruct((sources, 2, TOK), f32),
        jax.ShapeDtypeStruct((2, slots, D), bf16),
        jax.ShapeDtypeStruct((2, slots, D), bf16),
        jax.ShapeDtypeStruct((2, slots, FF), bf16),
        jax.ShapeDtypeStruct((2, slots, FF), bf16),
        jax.ShapeDtypeStruct((2, slots, FF), bf16),
    ]
    count = len(xs)
    out = pl.pallas_call(
        lambda *refs: expert_kernel(groups, *refs),
        out_shape=shapes,
        in_specs=[pl.BlockSpec(memory_space=pltpu.VMEM)] * (2 * count + 6),
        out_specs=[pl.BlockSpec(memory_space=pltpu.VMEM)] * len(shapes),
        compiler_params=pltpu.CompilerParams(vmem_limit_bytes=48 * 1024 * 1024),
        cost_estimate=pl.CostEstimate(
            flops=2 * 2 * slots * D * FF * 7, bytes_accessed=18_000_000, transcendentals=2 * slots * FF
        ),
    )(*xs, *cs, slot_lane, slot_col, gate_lane, gate_w, up_w, down_w)
    return out[:count], out[count:]


def output_kernel(groups, inner_ref, slot_col, down_w, *outs):
    rows = 2 * CAP
    lane_at = lax.broadcasted_iota(jnp.int32, (TOK, rows), 1)
    produced = [dot(inner_ref[e], down_w[e]) for e in range(2)]
    sources = [(g, k) for g in range(len(groups)) for k in range(groups[g])]
    for s, (g, k) in enumerate(sources):
        first, second = slot_col[s, :, 0:1], slot_col[s, :, 1:2] + CAP
        scatter = (lane_at == jnp.where(lane_at < CAP, first, second)).astype(f32).astype(bf16)
        span = slice(s * CAP, (s + 1) * CAP)
        part = jnp.concatenate([produced[0][span], produced[1][span]], axis=0).astype(bf16)
        outs[g][k * TOK : (k + 1) * TOK, :] = dot(scatter, part).astype(bf16)


def output_call(groups, inner, slot_col, down_w):
    shapes = [jax.ShapeDtypeStruct((g * TOK, D), bf16) for g in groups]
    return pl.pallas_call(
        lambda *refs: output_kernel(groups, *refs),
        out_shape=shapes,
        in_specs=[pl.BlockSpec(memory_space=pltpu.VMEM)] * 3,
        out_specs=[pl.BlockSpec(memory_space=pltpu.VMEM)] * len(shapes),
        compiler_params=pltpu.CompilerParams(vmem_limit_bytes=32 * 1024 * 1024),
        cost_estimate=pl.CostEstimate(
            flops=2 * 2 * inner.shape[1] * D * FF * 2, bytes_accessed=6_000_000, transcendentals=0
        ),
    )(inner, slot_col, down_w)


def gather_plane(block):
    line = jnp.concatenate([block] + [send_plane(block, 0, d) for d in (1, 2, 3)], axis=0)
    half = 2 * TOK
    one = send_plane(line, 1, 1)
    three = send_plane(line, 1, 3)
    two_low = send_plane(one[:half], 1, 1)
    two_high = send_plane(three[half:], 1, 3)
    return [line], [one], [two_low, two_high], [three]


def scatter_plane(own, one, two, three):
    half = 2 * TOK
    low = send_plane(two[0], 1, 3)
    high = send_plane(two[1], 1, 1)
    one = jnp.concatenate([(one[0][:half].astype(f32) + low.astype(f32)).astype(bf16), one[0][half:]], axis=0)
    three = jnp.concatenate([three[0][:half], (three[0][half:].astype(f32) + high.astype(f32)).astype(bf16)], axis=0)
    from_one = send_plane(one, 1, 3)
    from_three = send_plane(three, 1, 1)
    total = (own[0].astype(f32) + from_one.astype(f32) + from_three.astype(f32)).astype(bf16)
    parts = [total[d * TOK : (d + 1) * TOK] for d in range(RING)]
    parts = [parts[0]] + [send_plane(parts[d], 0, -d) for d in (1, 2, 3)]
    return sum(part.astype(f32) for part in parts)


def sum_plane(blocks, core, along, across):
    blocks = blocks.reshape((2, RING, RING) + blocks.shape[1:])
    other = send_core(pick(blocks, 1 - core))
    blocks = (pick(blocks, core).astype(f32) + other.astype(f32)).astype(bf16)
    for line, position in ((0, along), (1, across)):
        parts = [pick(blocks, position)]
        parts += [send_plane(pick(blocks, (position + d) % RING), line, d) for d in (1, 2, 3)]
        total = sum(part.astype(f32) for part in parts)
        blocks = total.astype(bf16)
    return total


def spread_plane(block, core, along, across):
    for line, position in ((1, across), (0, along)):
        block = in_order([block] + [send_plane(block, line, d) for d in (1, 2, 3)], position)
    other = send_core(block)
    low, high = jnp.where(core == 0, block, other), jnp.where(core == 0, other, block)
    both = jnp.stack([low, high])
    return both.reshape((EXPERTS,) + both.shape[3:])


def body(
    hidden,
    segments,
    routes,
    attention_gain,
    query_weight,
    key_weight,
    value_weight,
    projection_weight,
    mixture_gain,
    router_weight,
    gate_weight,
    up_weight,
    down_weight,
    cotangent,
):
    me = lax.axis_index("expert")
    mine = lax.axis_index("fsdp")
    core = me % 2
    chip = me // 2
    place_z, place_x = chip // RING, chip % RING
    along = jnp.where(core == 0, place_x, place_z)
    across = jnp.where(core == 0, place_z, place_x)
    groups = [[2 * i + c for i in range(EXPERTS // 2)] for c in range(2)]

    steps = jnp.arange(16, dtype=jnp.int32)
    from_across, from_along = (across - steps // RING) % RING, (along - steps % RING) % RING
    source_chip = jnp.where(core == 0, from_across * RING + from_along, from_along * RING + from_across)
    back_z, back_x = (place_z - steps // RING) % RING, (place_x - steps % RING) % RING
    source_step = jnp.where(core == 0, back_z * RING + back_x, back_x * RING + back_z)

    def trade(values):
        return lax.all_to_all(values, "expert", 0, 0, axis_index_groups=groups, tiled=True)

    hidden_blocks = [hidden] + [send_y(hidden, d) for d in (1, 2, 3)]
    segment_blocks = [segments] + [send_y(segments, d) for d in (1, 2, 3)]
    head_weights = jnp.concatenate(
        [w.reshape(256, RING, -1) for w in (query_weight, key_weight, value_weight)], axis=2
    ).transpose(1, 0, 2)
    own_heads = in_order(
        [pick(head_weights, mine)] + [send_y(pick(head_weights, (mine + d) % RING), d) for d in (1, 2, 3)], mine
    ).reshape(D, 512)
    gains = jnp.stack([attention_gain, mixture_gain])
    gains = in_order([gains] + [send_y(gains, d) for d in (1, 2, 3)], mine)
    gain_one = gains[:, 0].reshape(D).astype(f32)
    gain_two = gains[:, 1].reshape(D).astype(f32)

    named = (routes[:, :, None] == jnp.arange(EXPERTS, dtype=jnp.int32)[None, None, :]).astype(f32).sum(axis=1)
    lower = (jnp.arange(TOK)[:, None] > jnp.arange(TOK)[None, :]).astype(bf16)
    rank = dot(lower, named.astype(bf16)).astype(jnp.int32)
    slot = jnp.where(named > 0, rank, -1000)
    slot = trade(slot.T.reshape(16, 2, TOK))[source_chip]
    slot_lane = slot
    slot_col = slot.transpose(0, 2, 1)

    cot_blocks = gather_plane(cotangent)

    down_halves = down_weight[0].reshape(128, 2, 512).transpose(1, 0, 2).reshape(256, 512)
    pack = jnp.concatenate([gate_weight[0], up_weight[0], down_halves], axis=0)
    own_pack = in_order([pack] + [send_y(pack, d) for d in (1, 2, 3)], mine)
    other_pack = send_core(own_pack)
    packs = jnp.stack([jnp.where(core == 0, own_pack, other_pack), jnp.where(core == 0, other_pack, own_pack)])
    gate_full = packs[:, :, :256].reshape(2, D, FF)
    up_full = packs[:, :, 256:512].reshape(2, D, FF)
    down_full = packs[:, :, 512:].reshape(2, RING, 2, 128, 512).transpose(0, 1, 3, 2, 4).reshape(2, FF, D)

    projection = jnp.concatenate([projection_weight] + [send_y(projection_weight, -d) for d in (1, 2, 3)], axis=0)
    router = in_order([router_weight] + [send_y(router_weight, d) for d in (1, 2, 3)], mine).reshape(D, EXPERTS)

    x_all = jnp.concatenate(hidden_blocks, axis=0).astype(f32)
    segment_all = jnp.concatenate(segment_blocks, axis=0)
    order = (mine - jnp.arange(RING, dtype=jnp.int32)) % RING
    positions = (order[:, None] * TOK + jnp.arange(TOK, dtype=jnp.int32)[None, :]).reshape(-1)
    frequencies = base_theta ** (-2.0 * jnp.arange(HEAD // 2, dtype=jnp.int32).astype(f32) / HEAD)
    angles = positions.astype(f32)[:, None] * frequencies[None, :]
    angles = jnp.concatenate([angles, angles], axis=1)
    cosines, sines = jnp.cos(angles)[:, None, :], jnp.sin(angles)[:, None, :]
    scale_one = scale_of(x_all)
    activations = (x_all * scale_one * gain_one).astype(bf16)
    linear = dot(activations, own_heads)
    rows = RING * TOK
    queries = rotate(linear[:, :256].reshape(rows, 4, HEAD), cosines, sines).astype(bf16).reshape(rows, 2, 2, HEAD)
    keys = rotate(linear[:, 256:384].reshape(rows, 2, HEAD), cosines, sines).astype(bf16)
    values = linear[:, 384:].astype(bf16).reshape(rows, 2, HEAD)
    visible = (positions[None, :] <= positions[:, None]) & (segment_all[None, :] == segment_all[:, None])
    scaling = HEAD**-0.5
    scores = jnp.einsum("abyx,jbx->byaj", queries, keys, preferred_element_type=f32) * scaling
    scores = jnp.where(visible[None, None], scores, -1e30)
    exponents = jnp.exp(scores - jnp.max(scores, axis=-1, keepdims=True))
    unrounded = exponents / jnp.sum(exponents, axis=-1, keepdims=True)
    probabilities = unrounded.astype(bf16)
    mixed_heads = (
        jnp.einsum("icav,vie->aice", probabilities, values, preferred_element_type=f32)
        .reshape(rows, 256)
        .astype(bf16)
    )
    parts = [mixed_heads[r * TOK : (r + 1) * TOK] for r in range(RING)]
    mixed_rows = jnp.concatenate([parts[0]] + [send_y(parts[r], -r) for r in (1, 2, 3)], axis=1)
    residual = hidden.astype(f32)
    residual_two = residual + dot(mixed_rows, projection)
    scale_two = scale_of(residual_two)
    expert_input = (residual_two * scale_two * gain_two).astype(bf16)

    x_blocks = gather_plane(expert_input)
    logits = dot(expert_input, router)
    top_logit = jnp.max(jnp.where(named > 0, logits, -jnp.inf), axis=1, keepdims=True)
    gate_weights = jnp.where(named > 0, jnp.exp(jnp.where(named > 0, logits - top_logit, 0.0)), 0.0)
    gate_weights = gate_weights / jnp.sum(gate_weights, axis=1, keepdims=True)
    gate_lane = trade(gate_weights.T.reshape(16, 2, TOK))[source_chip]

    delta_parts, kept, out_parts = [], [], []
    for i in range(RING):
        span = slice(i * RING, (i + 1) * RING)
        delta_part, rest = expert_call(
            x_blocks[i], cot_blocks[i], slot_lane[span], slot_col[span], gate_lane[span], gate_full, up_full, down_full
        )
        delta_parts.append(delta_part)
        kept.append(rest)
    gate_delta = jnp.concatenate([rest[0] for rest in kept], axis=0)
    gate_delta = trade(gate_delta[source_step]).reshape(EXPERTS, TOK).T
    route_delta = scatter_plane(*delta_parts)
    for i in range(RING):
        span = slice(i * RING, (i + 1) * RING)
        sizes = tuple(x.shape[0] // TOK for x in x_blocks[i])
        out_parts.append(output_call(sizes, kept[i][3], slot_col[span], down_full))
    mixture = scatter_plane(*out_parts)
    output = (residual_two + mixture).astype(bf16)

    def expert_gradient(left, right):
        a = jnp.concatenate([rest[left] for rest in kept], axis=1)
        b = jnp.concatenate([rest[right] for rest in kept], axis=1)
        both = lax.dot_general(a, b, (((1,), (1,)), ((0,), (0,))), preferred_element_type=f32).astype(bf16)
        own = pick(both, core).astype(f32) + send_core(pick(both, 1 - core)).astype(f32)
        pieces = own.astype(bf16).reshape((RING, -1) + own.shape[1:])
        total = pick(pieces, mine).astype(f32)
        for d in (1, 2, 3):
            total = total + send_y(pick(pieces, (mine + d) % RING), d).astype(f32)
        return total[None]

    gate_gradient = expert_gradient(1, 4)
    up_gradient = expert_gradient(1, 5)
    down_gradient = expert_gradient(3, 2)

    mean_delta = jnp.sum(gate_weights * gate_delta, axis=1, keepdims=True)
    logit_delta = (gate_weights * (gate_delta - mean_delta)).astype(bf16)
    router_part = contract_rows(expert_input, logit_delta)
    input_delta = route_delta + contract_last(logit_delta, router)
    mixture_part = jnp.sum(input_delta * residual_two * scale_two, axis=0)
    inner = input_delta * gain_two
    upstream = cotangent.astype(f32)
    residual_delta = upstream + scale_two * (
        inner - residual_two * scale_two * scale_two * jnp.mean(inner * residual_two, axis=-1, keepdims=True)
    )
    attention_delta = residual_delta.astype(bf16)

    mixed_delta = contract_last(attention_delta, projection).astype(bf16)
    parts = [mixed_delta[:, r * 256 : (r + 1) * 256] for r in range(RING)]
    mixed_delta = jnp.concatenate([parts[0]] + [send_y(parts[r], r) for r in (1, 2, 3)], axis=0)
    mixed_delta = mixed_delta.reshape(rows, 2, 2, HEAD)
    probability_delta = jnp.einsum("abyx,jbx->byaj", mixed_delta, values, preferred_element_type=f32)
    row_delta = jnp.sum(probability_delta * unrounded, axis=-1, keepdims=True)
    score_delta = (unrounded * (probability_delta - row_delta)).astype(bf16)
    query_delta = jnp.einsum("icav,vie->aice", score_delta, keys, preferred_element_type=f32) * scaling
    key_delta = jnp.einsum("lapf,play->fly", score_delta, queries, preferred_element_type=f32) * scaling
    value_delta = jnp.einsum("lapf,play->fly", probabilities, mixed_delta, preferred_element_type=f32)
    query_delta = rotate_back(query_delta.reshape(rows, 4, HEAD), cosines, sines).reshape(rows, 256)
    key_delta = rotate_back(key_delta, cosines, sines).reshape(rows, 128)
    linear_delta = jnp.concatenate([query_delta, key_delta, value_delta.reshape(rows, 128)], axis=1).astype(bf16)

    attention_delta_all = jnp.concatenate(
        [attention_delta] + [send_y(attention_delta, d) for d in (1, 2, 3)], axis=0
    )
    projection_part = contract_rows(mixed_heads, attention_delta_all).astype(bf16)
    small = jnp.concatenate(
        [router_part, mixture_part[:, None], jnp.zeros((D, 128 - EXPERTS - 1), f32)], axis=1
    ).astype(bf16).reshape(RING, 256, 128)
    small = pick(small, mine).astype(f32) + sum(
        send_y(pick(small, (mine + d) % RING), d).astype(f32) for d in (1, 2, 3)
    )
    early = jnp.concatenate([projection_part, small.astype(bf16)], axis=1).reshape(EXPERTS, 8, D + 128)
    early = spread_plane(sum_plane(early, core, along, across).astype(bf16), core, along, across)
    early = early.reshape(256, D + 128).astype(f32)
    projection_gradient = early[:, :D]
    router_gradient = early[:, D : D + EXPERTS]
    mixture_gradient = early[:, D + EXPERTS]

    weight_part = contract_rows(activations, linear_delta)
    activation_part = contract_last(linear_delta, own_heads)
    gain_part = jnp.sum(activation_part * x_all * scale_one, axis=0)
    late = weight_part.reshape(RING, EXPERTS, 8, 512).transpose(1, 0, 2, 3).reshape(EXPERTS, 32, 512)
    gain_part = gain_part.reshape(RING, EXPERTS, 8).transpose(1, 0, 2)
    gain_rows = jnp.zeros((EXPERTS, 8, 512), f32).at[:, :RING, :8].set(gain_part)
    late = jnp.concatenate([late, gain_rows], axis=1).astype(bf16)
    late = sum_plane(late, core, along, across)
    pieces = jnp.concatenate(
        [late[:32].reshape(RING, 8, 512), jnp.broadcast_to(late[32:36, None], (RING, 8, 512))], axis=1
    ).astype(bf16)
    received = [pick(pieces, mine)] + [send_y(pick(pieces, (mine + d) % RING), d) for d in (1, 2, 3)]
    gain_sum = sum(part[8:].astype(f32) for part in received)
    pieces = in_order([part[:8] for part in received], mine).reshape(32, 512)
    late = spread_plane(jnp.concatenate([pieces, gain_sum.astype(bf16)], axis=0), core, along, across)
    attention_gradient = late[:, 32, :8].reshape(256).astype(f32)
    late = late[:, :32].reshape(EXPERTS, RING, 8, 512).transpose(0, 2, 1, 3).reshape(256, RING, 512).astype(f32)
    query_gradient = late[:, :, :256].reshape(256, D)
    key_gradient = late[:, :, 256:384].reshape(256, 512)
    value_gradient = late[:, :, 384:].reshape(256, 512)

    activation_part = activation_part.astype(bf16)
    parts = [activation_part[r * TOK : (r + 1) * TOK] for r in range(RING)]
    activation_delta = parts[0].astype(f32) + sum(send_y(parts[r], -r).astype(f32) for r in (1, 2, 3))
    own_scale = scale_one[:TOK]
    inner = activation_delta * gain_one
    input_gradient = residual_delta + own_scale * (
        inner - residual * own_scale * own_scale * jnp.mean(inner * residual, axis=-1, keepdims=True)
    )
    return (
        output,
        input_gradient,
        attention_gradient,
        query_gradient,
        key_gradient,
        value_gradient,
        projection_gradient,
        mixture_gradient,
        router_gradient,
        gate_gradient,
        up_gradient,
        down_gradient,
    )


def solution(mesh):
    rows = P(("expert", "fsdp"), None)
    weights = P("fsdp", None)
    experts = P("expert", "fsdp", None)
    return jax.shard_map(
        body,
        mesh=mesh,
        in_specs=(
            rows,
            P(("expert", "fsdp")),
            rows,
            P("fsdp"),
            weights,
            weights,
            weights,
            weights,
            P("fsdp"),
            weights,
            experts,
            experts,
            experts,
            rows,
        ),
        out_specs=(
            rows,
            rows,
            P("fsdp"),
            weights,
            weights,
            weights,
            weights,
            P("fsdp"),
            weights,
            experts,
            experts,
            experts,
        ),
        check_vma=False,
    )
```

time: 856 us -> 595 us (0.70)
  waiting for transfers between devices: 384 us -> 131 us
  blocking collectives: 204 us -> 0 us
  starting transfers between devices: 24.2 us -> 186 us
  matrix products: 105 us -> 55.4 us
  local copies, waits for them, and re-layouts: 64.3 us -> 106 us
  Pallas kernels: 0 us -> 41.5 us
  between operations: 17.3 us -> 3.32 us
  other arithmetic: 51.7 us -> 61.9 us
    reduce_scatter x8 -> x0, waiting for transfers between devices: 181 us -> none  [the longest x1 31.8 us: body(): lax.psum_scatter(projection_gradient.astype(jnp.bfloat16), 'fsdp', scatte...]
    ppermute x0 -> x108, starting transfers between devices: none -> 166 us  [the longest x48 84 us: send_y(): lax.ppermute(value, 'fsdp', [(i, (i + shift) % RING) for i in range(RING)])]
    psum x1 -> x0, blocking collectives: 126 us -> none  [body(): lax.psum(summed[0].astype(jnp.bfloat16), 'expert').astype(jnp.float32)]
    all_to_all x4 -> x3, waiting for transfers between devices: 135 us -> 25.7 us  [trade(): lax.all_to_all(values, 'expert', 0, 0, axis_index_groups=groups, tiled=True)]
    ppermute x0 -> x108, waiting for transfers between devices: none -> 105 us  [the longest x48 70 us: send_y(): lax.ppermute(value, 'fsdp', [(i, (i + shift) % RING) for i in range(RING)])]
    all_gather x5 -> x0, blocking collectives: 58.6 us -> none  [the longest x1 16.6 us: body(): lax.all_gather(value_row_block, 'fsdp', axis=0, tiled=True)]
    all_gather x7 -> x0, waiting for transfers between devices: 58.2 us -> none  [the longest x1 18.9 us: body(): lax.all_gather(projection_weight, 'fsdp', axis=0, tiled=True)]
    pallas_call x0 -> x8, Pallas kernels: none -> 41.5 us  [the longest x4 35.7 us: expert_call(): pl.pallas_call(lambda *refs: expert_kernel(groups, *refs), out_shape=shap...]
  transfers between devices with their start and end apart: 22 -> 111, of which waited for: 17 -> 42; matrix products, arithmetic and copies ran while one was open for 18% -> 31% of each run, Pallas kernels for 0% -> 5%
where the time goes in v1:
time: 595 us; the launch traced here: 585 us
  starting transfers between devices  186 us (31%)
  waiting for transfers between devices  131 us (22%)
  local copies, waits for them, and re-layouts  106 us (18%)
  other arithmetic  61.9 us (10%)
  matrix products  55.4 us (9%)
  Pallas kernels  41.5 us (7%)
    ppermute x48, starting transfers between devices, send_y(): lax.ppermute(value, 'fsdp', [(i, (i + shift) % RING) for i in range(RING)])  84 us
    ppermute x52, starting transfers between devices, send_plane(): return lax.ppermute(value, 'expert', plane_perm(line, shift % RING))  81.7 us
    ppermute x48, waiting for transfers between devices, send_y(): lax.ppermute(value, 'fsdp', [(i, (i + shift) % RING) for i in range(RING)])  70 us
    unnamed x329, local copies, waits for them, and re-layouts  56.7 us
    pallas_call x4, Pallas kernels, expert_call(): pl.pallas_call(lambda *refs: expert_kernel(groups, *refs), out_shape=shap...  35.7 us
    ppermute x52, waiting for transfers between devices, send_plane(): return lax.ppermute(value, 'expert', plane_perm(line, shift % RING))  34.9 us
    all_to_all x3, waiting for transfers between devices, trade(): lax.all_to_all(values, 'expert', 0, 0, axis_index_groups=groups, tiled=True)  25.7 us
    all_to_all x3, starting transfers between devices, trade(): lax.all_to_all(values, 'expert', 0, 0, axis_index_groups=groups, tiled=True)  19.6 us
  transfers between devices with their start and end apart: 111, of which 42 were waited for; matrix products, arithmetic and copies ran while one was open for 31% of the time, Pallas kernels for 5%

profile of v1, /device:TPU:0, one launch (start us, length us, event | category | flops | bytes accessed | tf_op | source)
XLA Modules:
  0.0 584.7 jit_solution(5379429687464865292)
XLA Ops:
  45.3 6.8 %collective-permute-done.24 = bf16[256,32]{0,1:T(8,128)(2,1)S(1)} collective-permute-done((bf16[256,32]{0,1:T(8,128)(2,1)}, bf16[256,32]{0,1:T(8,128)(2,1)S(1)}, u32[]{:S(2)}, u32[]{:S(2)}) %collective-permute-start.24) | collective-permute-done | bytes 16416 | tf_op jit(solution)/shard_map/ppermute | solution.py:51
  81.1 8.2 %fusion.191 = (f32[2,2,768]{2,1,0:T(2,128)S(1)}, f32[2,2,768,768]{2,3,1,0:T(8,128)}) fusion(bf16[768,2,64,1]{0,2,3,1:T(8,128)(2,1)} %fusion.129, bf16[768,2,2,64]{0,3,2,1:T(8,128)(2,1)} %fusion.95, pred[768,768]{0,1:T(8,128)(4,1)} %compare_and_fusion), kind=kOutput, calls=%fused_computation.449 | convolution fusion | flops 311427840 | bytes 10629120 | tf_op jit(solution)/shard_map/sub | solution.py:335
  89.3 4.8 fusion.78
  98.6 13.0 %collective-permute-done.27 = bf16[768,512]{1,0:T(8,128)(2,1)} collective-permute-done((bf16[768,512]{1,0:T(8,128)(2,1)}, bf16[768,512]{1,0:T(8,128)(2,1)}, u32[]{:S(2)}, u32[]{:S(2)}) %collective-permute-start.27) | collective-permute-done | bytes 786464 | tf_op jit(solution)/shard_map/ppermute | solution.py:51
  118.2 9.9 %collective-permute-start.12 = (bf16[192,256]{0,1:T(8,128)(2,1)S(1)}, bf16[192,256]{0,1:T(8,128)(2,1)S(1)}, u32[]{:S(2)}, u32[]{:S(2)}) collective-permute-start(bf16[192,256]{0,1:T(8,128)(2,1)S(1)} %bitcast.474), channel_id=1, source_target_pairs={{0,3},{1,0},{2,1},{3,2},{4,7},{5,4},{6,5},{7,6},{8,11},{9,8},{10,9... | collective-permute-start | bytes 294920 | tf_op jit(solution)/shard_map/ppermute | solution.py:51
  164.3 8.8 %all-to-all-start = ((s32[16,2,192]{2,1,0:T(2,128)}), s32[16,2,192]{2,1,0:T(2,128)S(1)}, u32[]{:S(2)}, u32[]{:S(2)}) async-start(s32[16,2,192]{2,1,0:T(2,128)} %reshape.714), calls=%async_computation | async-start | bytes 65536 | tf_op jit(solution)/shard_map/all_to_all | solution.py:279
  173.8 20.1 %all-to-all-done = s32[16,2,192]{2,1,0:T(2,128)S(1)} async-done(((s32[16,2,192]{2,1,0:T(2,128)}), s32[16,2,192]{2,1,0:T(2,128)S(1)}, u32[]{:S(2)}, u32[]{:S(2)}) %all-to-all-start) | async-done | bytes 24608 | tf_op jit(solution)/shard_map/all_to_all | solution.py:279
  194.0 7.3 %all-to-all-start.1 = ((f32[16,2,192]{2,1,0:T(2,128)}), f32[16,2,192]{2,1,0:T(2,128)S(1)}, u32[]{:S(2)}, u32[]{:S(2)}) async-start(f32[16,2,192]{2,1,0:T(2,128)} %reshape.716), calls=%async_computation.1 | async-start | bytes 65536 | tf_op jit(solution)/shard_map/all_to_all | solution.py:279
  203.3 5.5 all-to-all-done.1
  238.3 9.4 %shard_map.233 = (bf16[384,1024]{1,0:T(8,128)(2,1)}, bf16[384,1024]{1,0:T(8,128)(2,1)}, f32[4,2,192]{2,1,0:T(2,128)S(1)}, bf16[2,288,1024]{2,1,0:T(8,128)(2,1)},...) custom-call(bf16[384,1024]{1,0:T(8,128)(2,1)S(1)} %collective-permut, ...), custom_call_target="tpu_custom_call" | custom-call | flops 4227858432 | bytes 18000000 | tf_op jit(solution)/shard_map/pallas_call | solution.py:162
  253.5 8.6 %shard_map.229 = (bf16[768,1024]{1,0:T(8,128)(2,1)S(1)}, f32[4,2,192]{2,1,0:T(2,128)S(1)}, bf16[2,288,1024]{2,1,0:T(8,128)(2,1)S(1)}, bf16[2,288,1024]{2,1,0:T(8...) custom-call(bf16[768,1024]{1,0:T(8,128)(2,1)} %pad_maximum_fusion.2., ...), custom_call_target="tpu_custom_call" | custom-call | flops 4227858432 | bytes 18000000 | tf_op jit(solution)/shard_map/pallas_call | solution.py:162
  267.8 8.6 %shard_map.235 = (bf16[768,1024]{1,0:T(8,128)(2,1)S(1)}, f32[4,2,192]{2,1,0:T(2,128)S(1)}, bf16[2,288,1024]{2,1,0:T(8,128)(2,1)S(1)}, bf16[2,288,1024]{2,1,0:T(8...) custom-call(bf16[768,1024]{1,0:T(8,128)(2,1)} %collective-permute-do, ...), custom_call_target="tpu_custom_call" | custom-call | flops 4227858432 | bytes 18000000 | tf_op jit(solution)/shard_map/pallas_call | solution.py:162
  282.0 9.1 %shard_map.231 = (bf16[768,1024]{1,0:T(8,128)(2,1)S(1)}, f32[4,2,192]{2,1,0:T(2,128)S(1)}, bf16[2,288,1024]{2,1,0:T(8,128)(2,1)S(1)}, bf16[2,288,1024]{2,1,0:T(8...) custom-call(bf16[768,1024]{1,0:T(8,128)(2,1)} %collective-permute-do, ...), custom_call_target="tpu_custom_call" | custom-call | flops 4227858432 | bytes 18000000 | tf_op jit(solution)/shard_map/pallas_call | solution.py:162
  324.1 7.1 %fusion.55 = bf16[2,1024,512]{2,1,0:T(8,128)(2,1)S(1)} fusion(bf16[2,1152,1024]{2,1,0:T(8,128)(2,1)} %copy-done.103, bf16[2,288,512]{2,1,0:T(8,128)(2,1)S(1)} %copy-done.45, bf16[2,288,512]{2,1,0:T(8,128)(2,1)S(1)} %copy-done.39, bf16[2,288,512]{2,1,0:T(8,128)(2,1)S(1)} %copy-done.49, bf16[2,288,512]{2,1,0:T(8,128)(2,1)S(1)} %copy-done.43), kind=kOutput, calls=%fused_computation.81 | convolution fusion | flops 2426404864 | bytes 9175040 | tf_op jit(solution)/shard_map/dot_general | solution.py:378
  356.0 4.5 collective-permute-done.99
  385.3 4.9 collective-permute-start.105
  408.8 5.1 collective-permute-start.45
  419.2 5.5 collective-permute-start.78
  429.2 4.6 collective-permute-done.81
  447.6 6.0 %fusion.84 = bf16[2,64,768]{2,1,0:T(8,128)(2,1)} fusion(bf16[768,2,2,64]{0,3,2,1:T(8,128)(2,1)S(1)} %bitcast.463, f32[2,2,768,768]{2,3,1,0:T(8,128)} %get-tuple-element.242, f32[2,2,768]{2,1,0:T(2,128)S(1)} %copy-done.122), kind=kOutput, calls=%fused_computation.119 | convolution fusion | flops 306806784 | bytes 10039296 | tf_op jit(solution)/shard_map/lapf,play->fly/dot_general | solution.py:411
  453.6 6.8 %fusion.1 = (f32[2,2,768]{2,1,0:T(2,128)S(1)}, f32[2,768,768,2]{2,1,3,0:T(8,128)}) fusion(f32[2,2,768,768]{2,3,1,0:T(8,128)} %get-tuple-element.242, f32[2,2,768]{2,1,0:T(2,128)S(1)} %copy-done.122, bf16[768,2,64,1]{0,2,3,1:T(8,128)(2,1)S(1)} %bitcast.471, bf16[768,2,2,64]{0,3,2,1:T(8,128)(2,1)S(1)} %bitcast.464), kind=kOutput, calls=%fused_computation.6 | convolution fusion | flops 309064704 | bytes 19488768 | tf_op jit(solution)/shard_map/abyx,jbx->byaj/dot_general | solution.py:406
  460.4 10.0 %fusion.3 = bf16[2,2,768,768]{2,3,1,0:T(8,128)(2,1)} fusion(f32[2,768,768,2]{2,1,3,0:T(8,128)} %get-tuple-element.247, f32[2,2,768]{2,1,0:T(2,128)S(1)} %get-tuple-element.246, f32[2,2,768,768]{2,3,1,0:T(8,128)} %get-tuple-element.242, f32[2,2,768]{2,1,0:T(2,128)S(1)} %copy-done.122), kind=kLoop, calls=%fused_computation.8 | loop fusion | flops 9437184 | bytes 23617536 | tf_op jit(solution)/shard_map/convert_element_type | solution.py:408
  489.3 6.2 %collective-permute-done.58 = bf16[192,1024]{1,0:T(8,128)(2,1)} collective-permute-done((bf16[192,1024]{1,0:T(8,128)(2,1)}, bf16[192,1024]{1,0:T(8,128)(2,1)}, u32[]{:S(2)}, u32[]{:S(2)}) %collective-permute-start.58) | collective-permute-done | bytes 393248 | tf_op jit(solution)/shard_map/ppermute | solution.py:51
  536.2 4.7 collective-permute-done.93
  (733 shorter events, 396.0 us)
Async XLA Ops:
  33.2 38.8 %collective-permute-start.2 = (bf16[192,1024]{1,0:T(8,128)(2,1)S(1)}, bf16[192,1024]{1,0:T(8,128)(2,1)S(1)}, u32[]{:S(2)}, u32[]{:S(2)}) collective-permute-start(bf16[192,1024]{1,0:T(8,128)(2,1)S(1)} %copy-done.61), channel_id=1, source_target_pairs={{0,3},{1,0},{2,1},{3,2},{4,7},{5,4},{6,5},{7,6},{8,11},{9,8},{10,9... | collective-permute-start | bytes 1179656 | tf_op jit(solution)/shard_map/ppermute | solution.py:51
  36.3 37.2 %collective-permute-start.1 = (bf16[192,1024]{1,0:T(8,128)(2,1)S(1)}, bf16[192,1024]{1,0:T(8,128)(2,1)S(1)}, u32[]{:S(2)}, u32[]{:S(2)}) collective-permute-start(bf16[192,1024]{1,0:T(8,128)(2,1)S(1)} %copy-done.61), channel_id=1, source_target_pairs={{0,2},{1,3},{2,0},{3,1},{4,6},{5,7},{6,4},{7,5},{8,10},{9,11},{10,... | collective-permute-start | bytes 1179656 | tf_op jit(solution)/shard_map/ppermute | solution.py:51
  39.0 36.9 %collective-permute-start = (bf16[192,1024]{1,0:T(8,128)(2,1)S(1)}, bf16[192,1024]{1,0:T(8,128)(2,1)S(1)}, u32[]{:S(2)}, u32[]{:S(2)}) collective-permute-start(bf16[192,1024]{1,0:T(8,128)(2,1)S(1)} %copy-done.61), channel_id=1, source_target_pairs={{0,1},{1,2},{2,3},{3,0},{4,5},{5,6},{6,7},{7,4},{8,9},{9,10},{10,1... | collective-permute-start | bytes 1179656 | tf_op jit(solution)/shard_map/ppermute | solution.py:51
  72.0 39.6 %collective-permute-start.27 = (bf16[768,512]{1,0:T(8,128)(2,1)}, bf16[768,512]{1,0:T(8,128)(2,1)}, u32[]{:S(2)}, u32[]{:S(2)}) collective-permute-start(bf16[768,512]{1,0:T(8,128)(2,1)} %pad_maximum_fusion.9), channel_id=1, source_target_pairs={{0,3},{1,0},{2,1},{3,2},{4,7},{5,4},{6,5},{7,6},{8,11},{9,8},{10,9... | collective-permute-start | bytes 2359304 | tf_op jit(solution)/shard_map/ppermute | solution.py:51
  73.5 39.4 %collective-permute-start.28 = (bf16[768,512]{1,0:T(8,128)(2,1)}, bf16[768,512]{1,0:T(8,128)(2,1)}, u32[]{:S(2)}, u32[]{:S(2)}) collective-permute-start(bf16[768,512]{1,0:T(8,128)(2,1)} %pad_maximum_fusion.9), channel_id=1, source_target_pairs={{0,2},{1,3},{2,0},{3,1},{4,6},{5,7},{6,4},{7,5},{8,10},{9,11},{10,... | collective-permute-start | bytes 2359304 | tf_op jit(solution)/shard_map/ppermute | solution.py:51
  75.9 42.3 %collective-permute-start.29 = (bf16[768,512]{1,0:T(8,128)(2,1)}, bf16[768,512]{1,0:T(8,128)(2,1)}, u32[]{:S(2)}, u32[]{:S(2)}) collective-permute-start(bf16[768,512]{1,0:T(8,128)(2,1)} %pad_maximum_fusion.9), channel_id=1, source_target_pairs={{0,1},{1,2},{2,3},{3,0},{4,5},{5,6},{6,7},{7,4},{8,9},{9,10},{10,1... | collective-permute-start | bytes 2359304 | tf_op jit(solution)/shard_map/ppermute | solution.py:51
  94.3 41.9 %collective-permute-start.17 = (bf16[256,1024]{1,0:T(8,128)(2,1)S(1)}, bf16[256,1024]{1,0:T(8,128)(2,1)S(1)}, u32[]{:S(2)}, u32[]{:S(2)}) collective-permute-start(bf16[256,1024]{1,0:T(8,128)(2,1)S(1)} %copy-done.93), channel_id=1, source_target_pairs={{0,1},{1,2},{2,3},{3,0},{4,5},{5,6},{6,7},{7,4},{8,9},{9,10},{10,1... | collective-permute-start | bytes 1572872 | tf_op jit(solution)/shard_map/ppermute | solution.py:51
  96.0 46.5 %collective-permute-start.21 = (bf16[192,1024]{1,0:T(8,128)(2,1)S(1)}, bf16[192,1024]{1,0:T(8,128)(2,1)S(1)}, u32[]{:S(2)}, u32[]{:S(2)}) collective-permute-start(bf16[192,1024]{1,0:T(8,128)(2,1)S(1)} %copy-done.63), channel_id=1, source_target_pairs={{0,8},{4,36},{8,16},{12,44},{16,24},{20,52},{24,0},{28,60},{32,40}... | collective-permute-start | bytes 1179656 | tf_op jit(solution)/shard_map/ppermute | solution.py:43
  136.3 88.4 %collective-permute-start.30 = (bf16[4,768,512]{2,1,0:T(8,128)(2,1)}, bf16[4,768,512]{2,1,0:T(8,128)(2,1)}, u32[]{:S(2)}, u32[]{:S(2)}) collective-permute-start(bf16[4,768,512]{2,1,0:T(8,128)(2,1)} %constant_dynamic-slice_fusion.5), channel_id=1, source_target_pairs={{0,4},{4,0},{8,12},{12,8},{16,20},{20,16},{24,28},{28,24},{32,36},... | collective-permute-start | bytes 9437192 | tf_op jit(solution)/shard_map/ppermute | solution.py:47
  150.8 58.9 %collective-permute-start.32 = (bf16[768,1024]{1,0:T(8,128)(2,1)}, bf16[768,1024]{1,0:T(8,128)(2,1)}, u32[]{:S(2)}, u32[]{:S(2)}) collective-permute-start(bf16[768,1024]{1,0:T(8,128)(2,1)} %constant_dynamic-update-slice_fusion.11.refs_1_), channel_id=1, source_target_pairs={{0,32},{4,12},{8,40},{12,20},{16,48},{20,28},{24,56},{28,4},{32,64... | collective-permute-start | bytes 4718600 | tf_op jit(solution)/shard_map/ppermute | solution.py:43
  154.3 58.3 %collective-permute-start.37 = (bf16[768,1024]{1,0:T(8,128)(2,1)}, bf16[768,1024]{1,0:T(8,128)(2,1)}, u32[]{:S(2)}, u32[]{:S(2)}) collective-permute-start(bf16[768,1024]{1,0:T(8,128)(2,1)} %constant_dynamic-update-slice_fusion.11.refs_1_), channel_id=1, source_target_pairs={{0,96},{4,28},{8,104},{12,4},{16,112},{20,12},{24,120},{28,20},{32... | collective-permute-start | bytes 4718600 | tf_op jit(solution)/shard_map/ppermute | solution.py:43
  159.8 57.5 %collective-permute-start.31 = (bf16[768,1024]{1,0:T(8,128)(2,1)}, bf16[768,1024]{1,0:T(8,128)(2,1)}, u32[]{:S(2)}, u32[]{:S(2)}) collective-permute-start(bf16[768,1024]{1,0:T(8,128)(2,1)} %pad_maximum_fusion.2.refs_0_), channel_id=1, source_target_pairs={{0,32},{4,12},{8,40},{12,20},{16,48},{20,28},{24,56},{28,4},{32,64... | collective-permute-start | bytes 4718600 | tf_op jit(solution)/shard_map/ppermute | solution.py:43
  160.8 58.5 %collective-permute-start.34 = (bf16[768,1024]{1,0:T(8,128)(2,1)}, bf16[768,1024]{1,0:T(8,128)(2,1)}, u32[]{:S(2)}, u32[]{:S(2)}) collective-permute-start(bf16[768,1024]{1,0:T(8,128)(2,1)} %pad_maximum_fusion.2.refs_0_), channel_id=1, source_target_pairs={{0,96},{4,28},{8,104},{12,4},{16,112},{20,12},{24,120},{28,20},{32... | collective-permute-start | bytes 4718600 | tf_op jit(solution)/shard_map/ppermute | solution.py:43
  250.1 85.9 %collective-permute-start.48 = (bf16[384,1024]{1,0:T(8,128)(2,1)}, bf16[384,1024]{1,0:T(8,128)(2,1)}, u32[]{:S(2)}, u32[]{:S(2)}) collective-permute-start(bf16[384,1024]{1,0:T(8,128)(2,1)} %get-tuple-element.65), channel_id=1, source_target_pairs={{0,32},{4,12},{8,40},{12,20},{16,48},{20,28},{24,56},{28,4},{32,64... | collective-permute-start | bytes 2359304 | tf_op jit(solution)/shard_map/ppermute | solution.py:43
  250.3 89.2 %collective-permute-start.46 = (bf16[384,1024]{1,0:T(8,128)(2,1)}, bf16[384,1024]{1,0:T(8,128)(2,1)}, u32[]{:S(2)}, u32[]{:S(2)}) collective-permute-start(bf16[384,1024]{1,0:T(8,128)(2,1)} %get-tuple-element.63), channel_id=1, source_target_pairs={{0,96},{4,28},{8,104},{12,4},{16,112},{20,12},{24,120},{28,20},{32... | collective-permute-start | bytes 2359304 | tf_op jit(solution)/shard_map/ppermute | solution.py:43
  298.1 37.8 %all-to-all-start.2 = ((f32[16,2,192]{2,1,0:T(2,128)}), f32[16,2,192]{2,1,0:T(2,128)S(1)}, u32[]{:S(2)}, u32[]{:S(2)}) async-start(f32[16,2,192]{2,1,0:T(2,128)} %gather_fusion.2), calls=%async_computation.2 | async-start | bytes 65536 | tf_op jit(solution)/shard_map/all_to_all | solution.py:279
  305.8 37.5 %collective-permute-start.41 = (bf16[384,1024]{1,0:T(8,128)(2,1)}, bf16[384,1024]{1,0:T(8,128)(2,1)}, u32[]{:S(2)}, u32[]{:S(2)}) collective-permute-start(bf16[384,1024]{1,0:T(8,128)(2,1)} %get-tuple-element.60), channel_id=1, source_target_pairs={{0,32},{4,12},{8,40},{12,20},{16,48},{20,28},{24,56},{28,4},{32,64... | collective-permute-start | bytes 2359304 | tf_op jit(solution)/shard_map/ppermute | solution.py:43
  308.9 36.7 %collective-permute-start.39 = (bf16[384,1024]{1,0:T(8,128)(2,1)}, bf16[384,1024]{1,0:T(8,128)(2,1)}, u32[]{:S(2)}, u32[]{:S(2)}) collective-permute-start(bf16[384,1024]{1,0:T(8,128)(2,1)} %get-tuple-element.58), channel_id=1, source_target_pairs={{0,96},{4,28},{8,104},{12,4},{16,112},{20,12},{24,120},{28,20},{32... | collective-permute-start | bytes 2359304 | tf_op jit(solution)/shard_map/ppermute | solution.py:43
  343.3 55.0 %collective-permute-start.49 = (bf16[768,1024]{1,0:T(8,128)(2,1)}, bf16[768,1024]{1,0:T(8,128)(2,1)}, u32[]{:S(2)}, u32[]{:S(2)}) collective-permute-start(bf16[768,1024]{1,0:T(8,128)(2,1)} %pad_maximum_fusion.6), channel_id=1, source_target_pairs={{0,32},{4,12},{8,40},{12,20},{16,48},{20,28},{24,56},{28,4},{32,64... | collective-permute-start | bytes 4718600 | tf_op jit(solution)/shard_map/ppermute | solution.py:43
  345.6 52.8 %collective-permute-start.47 = (bf16[768,1024]{1,0:T(8,128)(2,1)}, bf16[768,1024]{1,0:T(8,128)(2,1)}, u32[]{:S(2)}, u32[]{:S(2)}) collective-permute-start(bf16[768,1024]{1,0:T(8,128)(2,1)} %pad_maximum_fusion.5), channel_id=1, source_target_pairs={{0,96},{4,28},{8,104},{12,4},{16,112},{20,12},{24,120},{28,20},{32... | collective-permute-start | bytes 4718600 | tf_op jit(solution)/shard_map/ppermute | solution.py:43
  408.8 103.7 %collective-permute-start.45 = (bf16[192,1024]{1,0:T(8,128)(2,1)}, bf16[192,1024]{1,0:T(8,128)(2,1)}, u32[]{:S(2)}, u32[]{:S(2)}) collective-permute-start(bf16[192,1024]{1,0:T(8,128)(2,1)} %get-tuple-element.167), channel_id=1, source_target_pairs={{0,8},{4,36},{8,16},{12,44},{16,24},{20,52},{24,0},{28,60},{32,40}... | collective-permute-start | bytes 1179656 | tf_op jit(solution)/shard_map/ppermute | solution.py:43
  419.2 64.5 %collective-permute-start.78 = (bf16[192,1024]{1,0:T(8,128)(2,1)}, bf16[192,1024]{1,0:T(8,128)(2,1)}, u32[]{:S(2)}, u32[]{:S(2)}) collective-permute-start(bf16[192,1024]{1,0:T(8,128)(2,1)} %fusion.181), channel_id=1, source_target_pairs={{0,3},{1,0},{2,1},{3,2},{4,7},{5,4},{6,5},{7,6},{8,11},{9,8},{10,9... | collective-permute-start | bytes 1179656 | tf_op jit(solution)/shard_map/ppermute | solution.py:51
  442.5 43.6 %collective-permute-start.77 = (bf16[192,1024]{1,0:T(8,128)(2,1)}, bf16[192,1024]{1,0:T(8,128)(2,1)}, u32[]{:S(2)}, u32[]{:S(2)}) collective-permute-start(bf16[192,1024]{1,0:T(8,128)(2,1)} %fusion.181), channel_id=1, source_target_pairs={{0,2},{1,3},{2,0},{3,1},{4,6},{5,7},{6,4},{7,5},{8,10},{9,11},{10,... | collective-permute-start | bytes 1179656 | tf_op jit(solution)/shard_map/ppermute | solution.py:51
  444.6 42.4 %collective-permute-start.76 = (bf16[192,1024]{1,0:T(8,128)(2,1)}, bf16[192,1024]{1,0:T(8,128)(2,1)}, u32[]{:S(2)}, u32[]{:S(2)}) collective-permute-start(bf16[192,1024]{1,0:T(8,128)(2,1)} %fusion.181), channel_id=1, source_target_pairs={{0,1},{1,2},{2,3},{3,0},{4,5},{5,6},{6,7},{7,4},{8,9},{9,10},{10,1... | collective-permute-start | bytes 1179656 | tf_op jit(solution)/shard_map/ppermute | solution.py:51
  (220 other events, 2132.9 us)
